TPU v7x, 128 devices: a whole 4x4x4 slice. The times are simulated.
128 devices in a mesh: row: 32 (over y, x_lo, z), col: 4 (over x_hi, core).
Axes of the slice: x: 4 (x_hi: 2, x_lo: 2; x = x_hi * 2 + x_lo), y: 4, z: 4, core: 2. Of those that a mesh axis runs over, the one named last changes fastest.
Arguments:
- features: bfloat16 [32768, 256], P('row', 'col'), may hold values from -6 to 6
- weight: bfloat16 [256, 256], replicated, may hold values from -0.375 to 0.375
- bias: float32 [256], P('col'), may hold values from -4 to 4
- edge_blocks: bfloat16 [32, 32, 16, 128, 128], P('row'), may hold values from 0.0003528595 to 0.03515625
- block_dst: int32 [32, 32, 16], P('row'), may hold values from 0 to 7
- block_src: int32 [32, 32, 16], P('row'), may hold values from 0 to 7
- counts: int32 [32, 32], P('row'), may hold values from 1 to 16, as said below
- cotangent: bfloat16 [32768, 256], P('row', 'col'), may hold values from -6 to 6
Outputs:
- output: bfloat16 [32768, 256], P('row', 'col')
- grad_input: bfloat16 [32768, 256], P('row', 'col')
- grad_weight: float32 [256, 256], P('col')
- grad_bias: float32 [256], P('col')
Inputs may be any that keep to these rules, and one draw needn't show every extreme that they name: `counts`: every panel's pair with itself has all 16 slots live.
All inputs are finite; a program needn't handle non-finite values.
Results may differ from a plain program's by a relative error of at most 0.008.
Values may be sent and summed in bfloat16 or wider, within the bound.
A program may use at most 128 MiB of HBM per device.

v0:
```python
import jax
import jax.numpy as jnp
from jax import lax
from jax.sharding import PartitionSpec as P


def forward_panel(blocks, src_ids, dst_ids, live_count, xpanel):
    size = blocks.shape[-1]
    slots = blocks.shape[0]
    group = min(4, slots)
    nblk = xpanel.shape[0] // size
    places = jnp.arange(nblk, dtype=jnp.int32)
    xblock = xpanel.reshape(nblk, size, -1)
    offsets = jnp.arange(group, dtype=jnp.int32)

    def forward_one_group(g, acc):
        first = g * group
        some_blocks = lax.dynamic_slice_in_dim(blocks, first, group, 0)
        some_src = lax.dynamic_slice_in_dim(src_ids, first, group, 0)
        some_dst = lax.dynamic_slice_in_dim(dst_ids, first, group, 0)
        live_k = first + offsets < live_count
        pick = (some_src[:, None] == places[None, :]).astype(jnp.bfloat16)
        chosen = jnp.einsum("kb,bnf->knf", pick, xblock, preferred_element_type=jnp.float32).astype(
            jnp.bfloat16
        )
        prods = jnp.einsum("kmn,knf->kmf", some_blocks, chosen, preferred_element_type=jnp.float32)
        put = ((some_dst[None, :] == places[:, None]) & live_k[None, :]).astype(jnp.float32)
        return acc + jnp.einsum("bk,kmf->bmf", put, prods, precision=lax.Precision.HIGHEST)

    groups = (live_count + group - 1) // group
    start = jnp.zeros((nblk, size, xpanel.shape[1]), jnp.float32)
    return lax.fori_loop(0, groups, forward_one_group, start).reshape(nblk * size, -1)


def adjoint_panel(blocks, src_ids, dst_ids, live_count, gpanel):
    size = blocks.shape[-1]
    slots = blocks.shape[0]
    group = min(4, slots)
    nblk = gpanel.shape[0] // size
    places = jnp.arange(nblk, dtype=jnp.int32)
    gblock = gpanel.reshape(nblk, size, -1)
    offsets = jnp.arange(group, dtype=jnp.int32)

    def adjoint_one_group(g, acc):
        first = g * group
        some_blocks = lax.dynamic_slice_in_dim(blocks, first, group, 0)
        some_src = lax.dynamic_slice_in_dim(src_ids, first, group, 0)
        some_dst = lax.dynamic_slice_in_dim(dst_ids, first, group, 0)
        live_k = first + offsets < live_count
        pick = ((some_dst[:, None] == places[None, :]) & live_k[:, None]).astype(jnp.bfloat16)
        chosen = jnp.einsum("kb,bmf->kmf", pick, gblock, preferred_element_type=jnp.float32).astype(
            jnp.bfloat16
        )
        prods = jnp.einsum("kmn,kmf->knf", some_blocks, chosen, preferred_element_type=jnp.float32)
        put = (some_src[None, :] == places[:, None]).astype(jnp.float32)
        return acc + jnp.einsum("bk,knf->bnf", put, prods, precision=lax.Precision.HIGHEST)

    groups = (live_count + group - 1) // group
    start = jnp.zeros((nblk, size, gpanel.shape[1]), jnp.float32)
    return lax.fori_loop(0, groups, adjoint_one_group, start).reshape(nblk * size, -1)


def pick_slot(table, index):
    return lax.dynamic_index_in_dim(table, index, 0, keepdims=False)


def body(features, weight, bias, edge_blocks, block_dst, block_src, counts, cotangent):
    panel_rows = features.shape[0]
    width_cols = features.shape[1]
    col_index = lax.axis_index("col")
    w_rows = lax.dynamic_slice_in_dim(weight, col_index * width_cols, width_cols, 0)
    w_cols = lax.dynamic_slice_in_dim(weight, col_index * width_cols, width_cols, 1)
    empty = jnp.zeros((panel_rows, width_cols), jnp.float32)
    blocks = edge_blocks[0]
    dst_ids = block_dst[0]
    src_ids = block_src[0]
    live = counts[0]
    piece = lax.all_gather(features, "row", axis=0, tiled=True)

    def add_one_panel(m, acc):
        xpanel = lax.dynamic_slice_in_dim(piece, m * panel_rows, panel_rows, 0)
        return acc + forward_panel(
            pick_slot(blocks, m),
            pick_slot(src_ids, m),
            pick_slot(dst_ids, m),
            pick_slot(live, m),
            xpanel,
        )

    agg_sum = lax.fori_loop(0, piece.shape[0] // panel_rows, add_one_panel, empty)
    aggregated = agg_sum.astype(jnp.bfloat16)
    agg_full = lax.all_gather(aggregated, "col", axis=1, tiled=True)
    pre = jnp.dot(agg_full, w_cols, preferred_element_type=jnp.float32) + bias
    output = jax.nn.silu(pre).astype(jnp.bfloat16)
    sig = jax.nn.sigmoid(pre)
    grad_pre = (cotangent.astype(jnp.float32) * sig * (1.0 + pre * (1.0 - sig))).astype(
        jnp.bfloat16
    )
    grad_full = lax.all_gather(grad_pre, "col", axis=1, tiled=True)
    grad_agg = lax.dot_general(
        grad_full, w_rows, (((1,), (1,)), ((), ())), preferred_element_type=jnp.float32
    ).astype(jnp.bfloat16)
    scale = 1.0 / (panel_rows * lax.axis_size("row")) ** 0.5
    weight_term = (
        lax.dot_general(
            aggregated, grad_full, (((0,), (0,)), ((), ())), preferred_element_type=jnp.float32
        )
        * scale
    )
    bias_term = jnp.sum(grad_pre.astype(jnp.float32), axis=0) * scale
    grad_weight, grad_bias = lax.psum((weight_term, bias_term), "row")

    def adjoint_one_panel(m):
        return adjoint_panel(
            pick_slot(blocks, m),
            pick_slot(src_ids, m),
            pick_slot(dst_ids, m),
            pick_slot(live, m),
            grad_agg,
        )

    parts = lax.map(
        adjoint_one_panel,
        jnp.arange(panel_rows * lax.axis_size("row") // panel_rows, dtype=jnp.int32),
    )
    grad_sum = lax.psum_scatter(
        parts.reshape(panel_rows * lax.axis_size("row"), width_cols),
        "row",
        scatter_dimension=0,
        tiled=True,
    )
    grad_input = grad_sum.astype(jnp.bfloat16)
    return (output, grad_input, grad_weight, grad_bias)


def solution(mesh):
    return jax.shard_map(
        body,
        mesh=mesh,
        in_specs=(
            P("row", "col"),
            P(),
            P("col"),
            P("row", None, None, None, None),
            P("row", None, None),
            P("row", None, None),
            P("row", None),
            P("row", "col"),
        ),
        out_specs=(P("row", "col"), P("row", "col"), P("col", None), P("col")),
        check_vma=False,
    )
```

profile of v0, /device:TPU:1, one launch (start us, length us, event | category | flops | bytes accessed | tf_op | source)
XLA Modules:
  0.0 1622.2 jit_solution(7532235211224599266)
XLA Ops:
  10.6 151.2 %all-gather.2.cloned.1.call-done = bf16[32768,64]{1,0:T(8,128)(2,1)} async-done(((bf16[1024,64]{1,0:T(8,128)(2,1)}), bf16[32768,64]{1,0:T(8,128)(2,1)}) %all-gather.2.cloned.1.call-update) | async-done | bytes 4194320 | tf_op jit(solution)/shard_map/all_gather | solution.py:78
  161.9 205.6 %while.116 = (s32[]{:T(128)}, f32[1024,64]{0,1:T(8,128)S(1)}, s32[32]{0:T(128)}, bf16[32,16,128,128]{3,2,1,0:T(8,128)(2,1)}, s32[32,16]{1,0:T(8,128)S(1)}, /*ind...) while((s32[]{:T(128)}, f32[1024,64]{0,1:T(8,128)S(1)}, ...), condition=%wide.region_3.4_spmd.clone, body=%wide.region_0.3_spmd.clone.sunk | while | flops 12255365 | bytes 3998770 | solution.py:90
  165.9 8.3 while.118
  367.5 27.1 %all_gather.10 = bf16[1024,256]{0,1:T(8,128)(2,1)S(1)} all-gather(bf16[1024,64]{0,1:T(8,128)(2,1)S(1)} %convert_element_type.31), channel_id=1, replica_groups=mesh['row'=32,'col'=4] {'col'}, dimensions={1}, use_global_device_ids=true | all-gather | bytes 655360 | tf_op jit(solution)/shard_map/all_gather | solution.py:92
  395.7 8.8 all_gather.11
  404.9 445.4 %while.114 = (s32[]{:T(128)}, f32[32,1024,64]{1,0,2:T(8,128)}, s32[32]{0:T(128)S(1)}, s32[32]{0:T(128)}, bf16[32,16,128,128]{3,2,1,0:T(8,128)(2,1)}, /*index=5*/...) while((s32[]{:T(128)}, f32[32,1024,64]{1,0,2:T(8,128)}, ...), condition=%wide.region_7.8_spmd, body=%wide.region_4.7_spmd.sunk | while | flops 12124291 | bytes 3474472 | solution.py:122
  410.5 8.3 while.117
  418.8 6.1 dynamic_update_slice.12
  432.5 6.1 dynamic_update_slice.12
  446.2 6.1 dynamic_update_slice.12
  460.0 6.1 dynamic_update_slice.12
  501.1 6.1 dynamic_update_slice.12
  638.3 6.1 dynamic_update_slice.12
  652.0 6.1 dynamic_update_slice.12
  665.8 6.1 dynamic_update_slice.12
  679.5 6.1 dynamic_update_slice.12
  693.2 6.1 dynamic_update_slice.12
  707.0 6.1 dynamic_update_slice.12
  720.7 6.1 dynamic_update_slice.12
  734.4 6.1 dynamic_update_slice.12
  850.3 11.7 copy.27
  863.0 389.9 %psum.15 = f32[64]{0:T(128)} all-reduce(f32[64]{0:T(128)S(1)} %broadcast_multiply_fusion), channel_id=1, replica_groups=mesh['row'=32,'col'=4] {'row'}, use_global_device_ids=true, to_apply=%region_11.12 | all-reduce | flops 64 | bytes 512 | tf_op jit(solution)/shard_map/psum | solution.py:111
  1252.9 83.3 %reduce-scatter.2.cloned.1.call-done = f32[1024,64]{0,1:T(8,128)} async-done(((f32[32768,64]{0,1:T(8,128)}), f32[1024,64]{0,1:T(8,128)}) %reduce-scatter.2.cloned.1.call-update) | async-done | bytes 262160 | tf_op jit(solution)/shard_map/reduce_scatter | solution.py:126
  1337.8 276.4 %all-reduce.2.cloned.1.call-done = f32[64,256]{1,0:T(8,128)} async-done(((f32[64,256]{1,0:T(8,128)}), f32[64,256]{1,0:T(8,128)}) %all-reduce.2.cloned.1.call-update) | async-done | bytes 65552 | tf_op jit(solution)/shard_map/psum | solution.py:111
  (1019 shorter events, 597.0 us)
Async XLA Ops:
  7.2 387.4 %copy-start = (bf16[256,256]{1,0:T(8,128)(2,1)S(1)}, bf16[256,256]{1,0:T(8,128)(2,1)}, u32[]{:S(2)}) copy-start(bf16[256,256]{1,0:T(8,128)(2,1)} %param.17) | copy-start | bytes 393220
  7.2 154.7 %all-gather.2.cloned.1.call-start = ((), (), s32[]{:S(2)}) async-start(), calls=%async_computation.1 | async-start | bytes 8650752 | tf_op jit(solution)/shard_map/all_gather | solution.py:78
  9.0 1327.1 %reduce-scatter.2.cloned.1.call-start = ((), (), s32[]{:S(2)}) async-start(), calls=%async_computation.2 | async-start | bytes 8650752 | tf_op jit(solution)/shard_map/reduce_scatter | solution.py:126
  161.9 232.7 %copy-start.1 = (bf16[1024,64]{0,1:T(8,128)(2,1)S(1)}, bf16[1024,64]{0,1:T(8,128)(2,1)}, u32[]{:S(2)}) copy-start(bf16[1024,64]{0,1:T(8,128)(2,1)} %param.23) | copy-start | bytes 393220
  161.9 232.7 %copy-start.2 = (f32[64]{0:T(128)S(1)}, f32[64]{0:T(128)}, u32[]{:S(2)}) copy-start(f32[64]{0:T(128)} %param.18) | copy-start | bytes 772
  862.0 752.2 %all-reduce.2.cloned.1.call-start = ((), (), s32[]{:S(2)}) async-start(), calls=%async_computation.3 | async-start | bytes 131072 | tf_op jit(solution)/shard_map/psum | solution.py:111
Sparse Core Ops, SparseCore 0:
  9.7 152.1 all-gather.1
  862.1 474.0 reduce-scatter.1
  1339.2 274.9 all-reduce.1
where the time goes:
time: 1650 us; the launch traced here: 1620 us
  waiting for transfers between devices  511 us (31%)
  local copies, waits for them, and re-layouts  443 us (27%)
  blocking collectives  426 us (26%)
  loops' own time  112 us (7%)
  matrix products  66.2 us (4%)
  other arithmetic  50.5 us (3%)
    psum x1, blocking collectives, body(): grad_weight, grad_bias = lax.psum((weight_term, bias_term), 'row')  390 us
    psum x1, waiting for transfers between devices, body(): grad_weight, grad_bias = lax.psum((weight_term, bias_term), 'row')  276 us
    dynamic_update_slice x32, local copies, waits for them, and re-layouts, body(): lax.map(adjoint_one_panel, jnp.arange(panel_rows * lax.axis_size('row') /...  194 us
    all_gather x1, waiting for transfers between devices, body(): piece = lax.all_gather(features, 'row', axis=0, tiled=True)  151 us
    another operation x1, loops' own time, body(): lax.map(adjoint_one_panel, jnp.arange(panel_rows * lax.axis_size('row') /...  84.7 us
    reduce_scatter x1, waiting for transfers between devices, body(): lax.psum_scatter(parts.reshape(panel_rows * lax.axis_size('row'), width_c...  83.3 us
    dynamic_slice x64, local copies, waits for them, and re-layouts, pick_slot(): return lax.dynamic_index_in_dim(table, index, 0, keepdims=False)  79.5 us
    squeeze x128, local copies, waits for them, and re-layouts, pick_slot(): return lax.dynamic_index_in_dim(table, index, 0, keepdims=False)  70.1 us
  transfers between devices with their start and end apart: 3, of which 3 were waited for; matrix products, arithmetic and copies ran while one was open for 0% of the time, Pallas kernels for 0%

commit v1 on v0

v1 whole, which is shorter than its diff:
```python
import functools

import jax
import jax.numpy as jnp
from jax import lax
from jax.experimental import pallas as pl
from jax.experimental.pallas import tpu as pltpu
from jax.sharding import PartitionSpec as P

MESH = pl.DeviceIdType.MESH
BF = jnp.bfloat16
F32 = jnp.float32

YP, YM, ZP, ZM = (1, 0), (-1, 0), (0, 1), (0, -1)


def _message(half, way, dy, dz):
    return (half, way, 4 * dy + dz, 4 * ((dy - way[0]) % 4) + (dz - way[1]) % 4)


ROUNDS = (
    (_message(0, YP, 0, 0), _message(0, YM, 0, 0), _message(1, ZP, 0, 0), _message(1, ZM, 0, 0)),
    (_message(1, YP, 0, 0), _message(1, YM, 0, 0), _message(0, ZP, 0, 0), _message(0, ZM, 0, 0)),
    (_message(0, YP, 3, 0), _message(1, YM, 0, 1), _message(1, ZP, 0, 3), _message(0, ZM, 1, 0)),
    (_message(1, YP, 0, 1), _message(1, YM, 0, 3), _message(0, ZP, 1, 0), _message(0, ZM, 3, 0)),
    (_message(1, YP, 0, 3), _message(1, YM, 0, 2), _message(0, ZP, 3, 0), _message(0, ZM, 2, 0)),
    (_message(1, YP, 0, 2), _message(1, YM, 1, 1), _message(0, ZP, 2, 0), _message(0, ZM, 1, 1)),
    (_message(1, YP, 3, 0), _message(1, YM, 1, 3), _message(0, ZP, 0, 3), _message(0, ZM, 3, 1)),
    (_message(1, YP, 3, 2), _message(0, ZP, 2, 3)),
)
NUMBER = {}
for _round in ROUNDS:
    for _m in _round:
        NUMBER[_m] = len(NUMBER)
MESSAGES = len(NUMBER)
SENT_FROM = {}
for _m in NUMBER:
    SENT_FROM.setdefault((_m[0], _m[2]), []).append(_m)

FEAT, COT, BIAS, PART, AGG, GRAD, OUT, WEIGHT, FINAL, END = 0, 2, 5, 8, 9, 10, 11, 12, 20, 22


def kernel(
    table,
    chain,
    feat,
    cot,
    weight,
    bias,
    edge,
    out_ref,
    gin_ref,
    gw_ref,
    gb_ref,
    blocks,
    blocks_t,
    gathered,
    acc,
    packed,
    swapped,
    cot_packed,
    cot_got,
    cot_full,
    bias_got,
    part_got,
    agg,
    pre_grad,
    grad_agg,
    out_half,
    wterm,
    wcore,
    wlink,
    wy,
    wz,
    shares,
    shares_got,
    final,
    final_got,
    edge_sem,
    send_sem,
    gather_sem,
    scatter_sem,
    odd_send,
    odd_recv,
):
    row, col = lax.axis_index("row"), lax.axis_index("col")
    y, a, z = row // 8, (row // 4) % 2, row % 4
    hi, b = col // 2, col % 2
    nslot = 16

    def device(yy, aa, zz, hh, bb):
        return ((yy * 2 + aa) * 4 + zz, hh * 2 + bb)

    def step(way):
        return device((y + way[0] + 4) % 4, a, (z + way[1] + 4) % 4, hi, b)

    def panel_of(slot):
        return (((y + slot // 4) % 4) * 2 + b) * 4 + (z + slot % 4) % 4

    loads = [
        pltpu.make_async_copy(
            edge.at[panel_of(s)], blocks.at[s, pl.ds(0, nslot)], edge_sem.at[s]
        )
        for s in range(nslot)
    ]
    for load in loads:
        load.start()

    partners = [device(y, 1 - a, z, hi, b), device(y, a, z, hi, 1 - b), device(y, 1 - a, z, hi, 1 - b)]
    partners += [device(y, a, z, 1 - hi, 0), device(y, a, z, 1 - hi, 1)]
    partners += [device((y + k) % 4, a, z, hi, b) for k in (1, 2, 3)]
    partners += [device(y, a, (z + k) % 4, hi, b) for k in (1, 2, 3)]
    barrier = pltpu.get_barrier_semaphore()
    for partner in partners:
        pl.semaphore_signal(barrier, inc=1, device_id=partner, device_id_type=MESH)

    packed[...] = jnp.concatenate([feat[:512, :], feat[512:, :]], axis=1)
    for half in range(2):
        cot_packed[half] = jnp.concatenate(
            [cot[half * 512 : half * 512 + 256, :], cot[half * 512 + 256 : half * 512 + 512, :]], axis=1
        )
    bias_row = bias[...]
    bias_got[col] = jnp.broadcast_to(jnp.concatenate([bias_row, bias_row], axis=1), (8, 128))
    pl.semaphore_wait(barrier, len(partners))

    def feature_copy(chip, core_from, target):
        return pltpu.make_async_remote_copy(
            src_ref=packed,
            dst_ref=swapped.at[core_from],
            send_sem=odd_send.at[FEAT + chip],
            recv_sem=odd_recv.at[FEAT + core_from],
            device_id=target,
            device_id_type=MESH,
        )

    for chip in range(2):
        here = jnp.logical_and(a == chip, a == b)

        @pl.when(jnp.logical_not(here))
        def _():
            feature_copy(chip, b, device(y, chip, z, hi, a)).start()

        @pl.when(here)
        def _():
            swapped[b] = packed[...]

    def cot_copy(k):
        other = (col + k) % 4
        return pltpu.make_async_remote_copy(
            src_ref=cot_packed.at[other % 2],
            dst_ref=cot_got.at[col],
            send_sem=odd_send.at[COT + k - 1],
            recv_sem=odd_recv.at[COT + k - 1],
            device_id=(row, other),
            device_id_type=MESH,
        )

    def cot_landed(k):
        return pltpu.make_async_remote_copy(
            src_ref=cot_packed.at[0],
            dst_ref=cot_got.at[(col + 4 - k) % 4],
            send_sem=odd_send.at[COT + k - 1],
            recv_sem=odd_recv.at[COT + k - 1],
            device_id=(row, (col + k) % 4),
            device_id_type=MESH,
        )

    def bias_copy(k, place):
        return pltpu.make_async_remote_copy(
            src_ref=bias_got.at[col],
            dst_ref=bias_got.at[place],
            send_sem=odd_send.at[BIAS + k - 1],
            recv_sem=odd_recv.at[BIAS + k - 1],
            device_id=(row, (col + k) % 4),
            device_id_type=MESH,
        )

    def merge(s):
        j = panel_of(s)
        blocks[s, nslot] = jnp.zeros((128, 128), BF)
        blocks_t[s, nslot] = jnp.zeros((128, 128), BF)

        def one(k, _):
            total = blocks[s, k] + blocks[s, chain[j * nslot + k]]
            blocks[s, k] = total
            blocks_t[s, k] = total.T
            return 0

        lax.fori_loop(0, nslot, one, 0)

    acc[...] = jnp.zeros_like(acc)
    for load in loads:
        load.wait()
    for s in range(nslot):
        merge(s)

    for core in range(2):

        @pl.when(jnp.logical_not(jnp.logical_and(a == b, core == b)))
        def _():
            feature_copy(0, core, device(y, 1 - a, z, hi, b)).wait_recv()

    first, second = swapped[0], swapped[1]
    gathered[0, 0] = jnp.concatenate([first[:, :64], second[:, :64]], axis=1)
    gathered[1, 0] = jnp.concatenate([first[:, 64:], second[:, 64:]], axis=1)

    def gather_copy(m):
        half, way, start, end = m
        return pltpu.make_async_remote_copy(
            src_ref=gathered.at[half, start],
            dst_ref=gathered.at[half, end],
            send_sem=send_sem.at[NUMBER[m]],
            recv_sem=gather_sem.at[NUMBER[m]],
            device_id=step(way),
            device_id_type=MESH,
        )

    def forward_unit(half, slot):
        j = panel_of(slot)

        def one(d, _):
            at = j * 64 + d * 8 + 4 * half
            lhs = jnp.concatenate([blocks[slot, table[at + s]] for s in range(4)], axis=1)
            acc[pl.ds(d * 128, 128), :] += jnp.dot(
                lhs, gathered[half, slot], preferred_element_type=F32
            )
            return 0

        lax.fori_loop(0, 8, one, 0)

    for m in ROUNDS[0] + ROUNDS[1]:
        gather_copy(m).start()
    for k in (1, 2, 3):
        cot_copy(k).start()
        bias_copy(k, col).start()
    cot_got[col] = cot_packed[b]
    forward_unit(0, 0)
    forward_unit(1, 0)
    for k, now in enumerate(ROUNDS):
        for m in now:
            gather_copy(m).wait_recv()
        if k + 2 < len(ROUNDS):
            for m in ROUNDS[k + 2]:
                gather_copy(m).start()
        for m in now:
            forward_unit(m[0], m[3])
        if k == 4:
            for other in (1, 2, 3):
                cot_landed(other).wait_recv()
                bias_copy(other, (col + 4 - other) % 4).wait_recv()
            cot_full[:256, :] = jnp.concatenate([cot_got[c][:, :64] for c in range(4)], axis=1)
            cot_full[256:, :] = jnp.concatenate([cot_got[c][:, 64:] for c in range(4)], axis=1)

    mine = pl.multiple_of(b * 512, 512)
    theirs = pl.multiple_of(512 - b * 512, 512)
    sibling = device(y, a, z, hi, 1 - b)
    part_copy = pltpu.make_async_remote_copy(
        src_ref=acc.at[pl.ds(theirs, 512)],
        dst_ref=part_got,
        send_sem=odd_send.at[PART],
        recv_sem=odd_recv.at[PART],
        device_id=sibling,
        device_id_type=MESH,
    )
    part_copy.start()
    for m in NUMBER:
        gather_copy(m).wait_send()
    part_copy.wait_recv()
    agg[hi] = (acc[pl.ds(mine, 512), :] + part_got[...]).astype(BF)
    agg_copy = pltpu.make_async_remote_copy(
        src_ref=agg.at[hi],
        dst_ref=agg.at[hi],
        send_sem=odd_send.at[AGG],
        recv_sem=odd_recv.at[AGG],
        device_id=device(y, a, z, 1 - hi, b),
        device_id_type=MESH,
    )
    agg_copy.start()
    agg_landed = pltpu.make_async_remote_copy(
        src_ref=agg.at[hi],
        dst_ref=agg.at[1 - hi],
        send_sem=odd_send.at[AGG],
        recv_sem=odd_recv.at[AGG],
        device_id=device(y, a, z, 1 - hi, b),
        device_id_type=MESH,
    )
    bias_all = jnp.concatenate([bias_got[c][0:1, :64] for c in range(4)], axis=1)
    agg_landed.wait_recv()

    def dense(t, bias_sum):
        at = pl.ds(pl.multiple_of(t * 128, 128), 128)
        pre = jnp.dot(agg[0, at, :], weight[:128, :], preferred_element_type=F32)
        pre += jnp.dot(agg[1, at, :], weight[128:, :], preferred_element_type=F32)
        pre += bias_all
        sig = jax.nn.sigmoid(pre)
        value = pre * sig
        out_half[b, at, :] = jnp.where(hi == 0, value[:, :128], value[:, 128:]).astype(BF)
        grad = (cot_full[at, :].astype(F32) * sig * (1.0 + pre * (1.0 - sig))).astype(BF)
        pre_grad[at, :] = grad
        grad_agg[b, at, :] = lax.dot_general(
            grad,
            weight[pl.ds(pl.multiple_of(hi * 128, 128), 128), :],
            (((1,), (1,)), ((), ())),
            preferred_element_type=F32,
        ).astype(BF)
        return bias_sum + jnp.sum(grad.astype(F32), axis=0, keepdims=True)

    bias_sum = lax.fori_loop(0, 4, dense, jnp.zeros((1, 256), F32))

    def pair_copy(ref, place, n):
        return pltpu.make_async_remote_copy(
            src_ref=ref.at[b],
            dst_ref=ref.at[place],
            send_sem=odd_send.at[n],
            recv_sem=odd_recv.at[n],
            device_id=sibling,
            device_id_type=MESH,
        )

    pair_copy(grad_agg, b, GRAD).start()
    pair_copy(out_half, b, OUT).start()

    term = lax.dot_general(
        agg[hi], pre_grad[...], (((0,), (0,)), ((), ())), preferred_element_type=F32
    )
    for core in range(2):
        wterm[core, :64] = term[core * 64 : core * 64 + 64, :]
        wterm[core, 64:] = jnp.broadcast_to(bias_sum, (8, 256))

    def weight_copy(src, dst, target, n):
        return pltpu.make_async_remote_copy(
            src_ref=src,
            dst_ref=dst,
            send_sem=odd_send.at[WEIGHT + n],
            recv_sem=odd_recv.at[WEIGHT + n],
            device_id=target,
            device_id_type=MESH,
        )

    weight_core = weight_copy(wterm.at[1 - b], wcore, sibling, 0)
    weight_core.start()
    weight_link = weight_copy(wlink.at[0], wlink.at[1], device(y, 1 - a, z, hi, b), 1)

    def weight_y(k, place):
        return weight_copy(wy.at[y], wy.at[place], device((y + k) % 4, a, z, hi, b), 1 + k)

    def weight_z(k, place):
        return weight_copy(wz.at[z], wz.at[place], device(y, a, (z + k) % 4, hi, b), 4 + k)

    def scatter_copy(m):
        half, way, start, end = m
        return pltpu.make_async_remote_copy(
            src_ref=shares.at[half, end],
            dst_ref=shares_got.at[NUMBER[m]],
            send_sem=send_sem.at[NUMBER[m]],
            recv_sem=scatter_sem.at[NUMBER[m]],
            device_id=step((-way[0], -way[1])),
            device_id_type=MESH,
        )

    def backward_unit(half, slot, keep):
        j = panel_of(slot)
        came = SENT_FROM.get((half, slot), ())
        for m in came:
            scatter_copy(m).wait_recv()

        def one(s, _):
            at = j * 64 + 4 * half + s
            total = jnp.zeros((128, 128), F32)
            for h in range(2):
                lhs = jnp.concatenate(
                    [blocks_t[slot, table[at + 8 * (4 * h + d)]] for d in range(4)], axis=1
                )
                total += jnp.dot(lhs, grad_agg[h], preferred_element_type=F32)
            rows = pl.ds(pl.multiple_of(s * 128, 128), 128)
            for m in came:
                total += shares_got[NUMBER[m], rows, :].astype(F32)
            keep(rows, total)
            return 0

        lax.fori_loop(0, 4, one, 0)

    pair_copy(grad_agg, 1 - b, GRAD).wait_recv()
    for k in range(len(ROUNDS) - 1, -1, -1):
        for m in ROUNDS[k]:
            half, end = m[0], m[3]

            def keep(rows, total):
                shares[half, end, rows, :] = total.astype(BF)

            backward_unit(half, end, keep)
            scatter_copy(m).start()
        if k == 7:
            weight_core.wait_recv()
            wlink[0] = wterm[b] + wcore[...]
            weight_link.start()
        if k == 5:
            weight_link.wait_recv()
            wy[y] = wlink[0] + wlink[1]
            for n in (1, 2, 3):
                weight_y(n, y).start()
        if k == 2:
            for n in (1, 2, 3):
                weight_y(n, (y + 4 - n) % 4).wait_recv()
            wz[z] = (wy[0] + wy[1]) + (wy[2] + wy[3])
            for n in (1, 2, 3):
                weight_z(n, z).start()

    pair_copy(out_half, 1 - b, OUT).wait_recv()
    for half in range(2):
        both = out_half[half]
        out_ref[half * 512 : half * 512 + 512, :] = jnp.where(b == 0, both[:, :64], both[:, 64:])

    for half in range(2):

        def keep_final(rows, total):
            shares[half, 0, rows, :] = total.astype(BF)

        backward_unit(half, 0, keep_final)
    low, high = shares[0, 0], shares[1, 0]
    final[0] = jnp.concatenate([low[:, :64], high[:, :64]], axis=1)
    final[1] = jnp.concatenate([low[:, 64:], high[:, 64:]], axis=1)

    def final_copy(core, chip_from, target):
        return pltpu.make_async_remote_copy(
            src_ref=final.at[core],
            dst_ref=final_got.at[chip_from],
            send_sem=odd_send.at[FINAL + core],
            recv_sem=odd_recv.at[FINAL + chip_from],
            device_id=target,
            device_id_type=MESH,
        )

    for core in range(2):
        here = jnp.logical_and(a == b, b == core)

        @pl.when(jnp.logical_not(here))
        def _():
            final_copy(core, a, device(y, b, z, hi, core)).start()

        @pl.when(here)
        def _():
            final_got[a] = final[core]

    for n in (1, 2, 3):
        weight_z(n, (z + 4 - n) % 4).wait_recv()
    scale = 1.0 / (32 * 1024) ** 0.5
    whole = ((wz[0] + wz[1]) + (wz[2] + wz[3])) * scale
    gw_ref[...] = whole[:64, :]
    gb = whole[64:65, :]
    own = jnp.where(hi == 0, gb[:, :128], gb[:, 128:])
    gb_ref[...] = jnp.where(b == 0, own[:, :64], own[:, 64:])

    for chip in range(2):

        @pl.when(jnp.logical_not(jnp.logical_and(a == b, chip == a)))
        def _():
            final_copy(0, chip, device(y, 1 - a, z, hi, b)).wait_recv()

    total = (final_got[0].astype(F32) + final_got[1].astype(F32)).astype(BF)
    gin_ref[:512, :] = total[:, :64]
    gin_ref[512:, :] = total[:, 64:]

    for chip in range(2):

        @pl.when(jnp.logical_not(jnp.logical_and(a == chip, a == b)))
        def _():
            feature_copy(chip, b, device(y, chip, z, hi, a)).wait_send()

    for k in (1, 2, 3):
        cot_copy(k).wait_send()
        bias_copy(k, col).wait_send()
        weight_y(k, y).wait_send()
        weight_z(k, z).wait_send()
    part_copy.wait_send()
    agg_copy.wait_send()
    pair_copy(grad_agg, b, GRAD).wait_send()
    pair_copy(out_half, b, OUT).wait_send()
    weight_core.wait_send()
    weight_link.wait_send()
    for m in NUMBER:
        scatter_copy(m).wait_send()
    for core in range(2):

        @pl.when(jnp.logical_not(jnp.logical_and(a == b, b == core)))
        def _():
            final_copy(core, a, device(y, b, z, hi, core)).wait_send()


def slot_tables(block_dst, block_src, counts):
    slots = block_dst.shape[1]
    k = jnp.arange(slots, dtype=jnp.int32)
    live = k[None, :] < counts[:, None]
    cell = jnp.where(live, block_dst * 8 + block_src, -1)
    places = jnp.arange(64, dtype=jnp.int32)
    hit = cell[:, None, :] == places[None, :, None]
    table = jnp.max(jnp.where(hit, k[None, None, :], -1), axis=2)
    table = jnp.where(table < 0, slots, table)
    before = (cell[:, None, :] == cell[:, :, None]) & (k[None, None, :] < k[None, :, None])
    chain = jnp.max(jnp.where(before & live[:, :, None], k[None, None, :], -1), axis=2)
    chain = jnp.where(chain < 0, slots, chain)
    return table.reshape(-1), chain.reshape(-1)


def body(features, weight, bias, edge_blocks, block_dst, block_src, counts, cotangent):
    table, chain = slot_tables(block_dst[0], block_src[0], counts[0])
    vmem = pl.BlockSpec(memory_space=pltpu.VMEM)
    smem = pl.BlockSpec(memory_space=pltpu.SMEM)
    out, gin, gw, gb = pl.pallas_call(
        kernel,
        out_shape=(
            jax.ShapeDtypeStruct((1024, 64), BF),
            jax.ShapeDtypeStruct((1024, 64), BF),
            jax.ShapeDtypeStruct((64, 256), F32),
            jax.ShapeDtypeStruct((1, 64), F32),
        ),
        in_specs=[smem, smem, vmem, vmem, vmem, vmem, pl.BlockSpec(memory_space=pl.ANY)],
        out_specs=(vmem, vmem, vmem, vmem),
        scratch_shapes=[
            pltpu.VMEM((16, 17, 128, 128), BF),
            pltpu.VMEM((16, 17, 128, 128), BF),
            pltpu.VMEM((2, 16, 512, 128), BF),
            pltpu.VMEM((1024, 128), F32),
            pltpu.VMEM((512, 128), BF),
            pltpu.VMEM((2, 512, 128), BF),
            pltpu.VMEM((2, 256, 128), BF),
            pltpu.VMEM((4, 256, 128), BF),
            pltpu.VMEM((512, 256), BF),
            pltpu.VMEM((4, 8, 128), F32),
            pltpu.VMEM((512, 128), F32),
            pltpu.VMEM((2, 512, 128), BF),
            pltpu.VMEM((512, 256), BF),
            pltpu.VMEM((2, 512, 128), BF),
            pltpu.VMEM((2, 512, 128), BF),
            pltpu.VMEM((2, 72, 256), F32),
            pltpu.VMEM((72, 256), F32),
            pltpu.VMEM((2, 72, 256), F32),
            pltpu.VMEM((4, 72, 256), F32),
            pltpu.VMEM((4, 72, 256), F32),
            pltpu.VMEM((2, 16, 512, 128), BF),
            pltpu.VMEM((MESSAGES, 512, 128), BF),
            pltpu.VMEM((2, 512, 128), BF),
            pltpu.VMEM((2, 512, 128), BF),
            pltpu.SemaphoreType.DMA((16,)),
            pltpu.SemaphoreType.DMA((MESSAGES,)),
            pltpu.SemaphoreType.DMA((MESSAGES,)),
            pltpu.SemaphoreType.DMA((MESSAGES,)),
            pltpu.SemaphoreType.DMA((END,)),
            pltpu.SemaphoreType.DMA((END,)),
        ],
        compiler_params=pltpu.CompilerParams(
            collective_id=0, has_side_effects=True, vmem_limit_bytes=56 * 1024 * 1024
        ),
        name="graph_layer",
    )(table, chain, features, cotangent, weight, bias.reshape(1, 64), edge_blocks[0])
    return out, gin, gw, gb.reshape(64)


def solution(mesh):
    return jax.shard_map(
        body,
        mesh=mesh,
        in_specs=(
            P("row", "col"),
            P(),
            P("col"),
            P("row", None, None, None, None),
            P("row", None, None),
            P("row", None, None),
            P("row", None),
            P("row", "col"),
        ),
        out_specs=(P("row", "col"), P("row", "col"), P("col", None), P("col")),
        check_vma=False,
    )
```

time: 1650 us -> 143 us (0.09); the launches traced: 1620 us -> 142 us
  waiting for transfers between devices: 511 us -> 0 us
  local copies, waits for them, and re-layouts: 443 us -> 9.79 us
  blocking collectives: 426 us -> 0 us
  Pallas kernels: 0 us -> 129 us
  loops' own time: 112 us -> 0 us
  matrix products: 66.2 us -> 0 us
  other arithmetic: 50.5 us -> 2.88 us
    psum x1 -> x0, blocking collectives: 390 us -> none  [body(): grad_weight, grad_bias = lax.psum((weight_term, bias_term), 'row')]
    psum x1 -> x0, waiting for transfers between devices: 276 us -> none  [body(): grad_weight, grad_bias = lax.psum((weight_term, bias_term), 'row')]
    dynamic_update_slice x32 -> x0, local copies, waits for them, and re-layouts: 194 us -> none  [body(): lax.map(adjoint_one_panel, jnp.arange(panel_rows * lax.axis_size('row') /...]
    all_gather x1 -> x0, waiting for transfers between devices: 151 us -> none  [body(): piece = lax.all_gather(features, 'row', axis=0, tiled=True)]
    dynamic_slice x268 -> x0, local copies, waits for them, and re-layouts: 140 us -> none  [the longest x64 79.5 us: pick_slot(): return lax.dynamic_index_in_dim(table, index, 0, keepdims=False)]
    pallas_call x0 -> x1, Pallas kernels: none -> 129 us  [body(): pl.pallas_call(kernel, out_shape=(jax.ShapeDtypeStruct((1024, 64), BF), j...]
    another operation x66 -> x0, loops' own time: 112 us -> none  [the longest x1 84.7 us: body(): lax.map(adjoint_one_panel, jnp.arange(panel_rows * lax.axis_size('row') /...]
    reduce_scatter x1 -> x0, waiting for transfers between devices: 83.3 us -> none  [body(): lax.psum_scatter(parts.reshape(panel_rows * lax.axis_size('row'), width_c...]
  transfers between devices with their start and end apart: 3 -> 0, of which waited for: 3 -> 0; matrix products, arithmetic and copies ran while one was open for 0% -> 0% of each run, Pallas kernels for 0% -> 0%
where the time goes in v1:
time: 143 us; the launch traced here: 142 us
  Pallas kernels  129 us (90%)
  local copies, waits for them, and re-layouts  9.79 us (7%)
  other arithmetic  2.88 us (2%)
    pallas_call x1, Pallas kernels, body(): pl.pallas_call(kernel, out_shape=(jax.ShapeDtypeStruct((1024, 64), BF), j...  129 us
    unnamed x6, local copies, waits for them, and re-layouts  9.49 us

profile of v1, /device:TPU:1, one launch (start us, length us, event | category | flops | bytes accessed | tf_op | source)
XLA Modules:
  0.0 142.4 jit_solution(18096768424892723285)
XLA Ops:
  0.6 0.7 iota_compare_fusion.2
  1.3 0.7 bitcast_select_fusion
  2.0 0.1 select_reduce_fusion.1
  2.2 0.1 copy.28
  2.2 0.2 select_reduce_fusion
  2.4 0.1 reduce_max.23
  2.5 0.6 compare_select_fusion.table
  3.1 0.1 copy.29
  3.2 0.1 reduce_max.25
  3.2 0.6 compare_select_fusion.1.chain
  3.8 1.7 %copy.30.feat = bf16[1024,64]{1,0:T(8,128)(2,1)} copy(bf16[1024,64]{0,1:T(8,128)(2,1)} %param.8) | data formatting | bytes 262144 | tf_op args[0]
  5.6 1.7 %copy.31.cot = bf16[1024,64]{1,0:T(8,128)(2,1)} copy(bf16[1024,64]{0,1:T(8,128)(2,1)} %param.15) | data formatting | bytes 262144 | tf_op args[7]
  7.3 129.0 %graph_layer.1 = (bf16[1024,64]{1,0:T(8,128)(2,1)}, bf16[1024,64]{1,0:T(8,128)(2,1)}, f32[64,256]{1,0:T(8,128)}, f32[1,64]{1,0:T(1,128)}) custom-call(s32[2048]{0:T(1024)} %compare_select_fusion.table, s32[512]{0:T(512)} %compare_select_fusion.1.chain, bf16[1024,64]{1,0:T(8,128)(2,1)} %copy.30.feat, bf16[1024,64]{1,0:T(8,128)(2,1)} %copy.31.cot, ...), custom_call_target="tpu_custom_call" | custom-call | tf_op jit(solution)/shard_map/graph_layer/pallas_call | solution.py:509
  136.4 1.7 %copy.32 = bf16[1024,64]{0,1:T(8,128)(2,1)} copy(bf16[1024,64]{1,0:T(8,128)(2,1)} %get-tuple-element.20) | data formatting | bytes 262144
  138.1 1.7 %copy.33 = bf16[1024,64]{0,1:T(8,128)(2,1)} copy(bf16[1024,64]{1,0:T(8,128)(2,1)} %get-tuple-element.21) | data formatting | bytes 262144
  139.8 1.5 %copy.36 = f32[64,256]{1,0:T(8,128)} copy(f32[64,256]{1,0:T(8,128)} %get-tuple-element.30) | data formatting | bytes 131072
  141.3 1.1 copy.37
  (1 shorter events, 0.0 us)

commit v2 on v0

v2 whole, which is shorter than its diff:
```python
import functools

import jax
import jax.numpy as jnp
from jax import lax
from jax.experimental import pallas as pl
from jax.experimental.pallas import tpu as pltpu
from jax.sharding import PartitionSpec as P

MESH = pl.DeviceIdType.MESH
BF = jnp.bfloat16
F32 = jnp.float32

YP, YM, ZP, ZM = (1, 0), (-1, 0), (0, 1), (0, -1)


def _message(half, way, dy, dz):
    return (half, way, 4 * dy + dz, 4 * ((dy - way[0]) % 4) + (dz - way[1]) % 4)


ROUNDS = (
    (_message(0, YP, 0, 0), _message(0, YM, 0, 0), _message(0, ZP, 0, 0), _message(0, ZM, 0, 0)),
    (_message(1, ZP, 0, 0), _message(1, ZM, 0, 0), _message(1, YP, 0, 0), _message(1, YM, 0, 0)),
    (_message(0, YP, 3, 0), _message(0, ZP, 1, 0), _message(0, ZM, 1, 0)),
    (_message(1, YP, 0, 1), _message(1, YM, 0, 1), _message(1, ZP, 0, 3), _message(0, ZM, 3, 0)),
    (_message(1, YP, 0, 3), _message(1, YM, 0, 3), _message(0, ZP, 3, 0), _message(0, ZM, 2, 0)),
    (_message(1, YP, 0, 2), _message(1, YM, 0, 2), _message(0, ZP, 2, 0), _message(0, ZM, 1, 1)),
    (_message(1, YP, 3, 0), _message(1, YM, 1, 1), _message(0, ZP, 0, 3), _message(0, ZM, 3, 1)),
    (_message(1, YP, 3, 2), _message(1, YM, 1, 3), _message(0, ZP, 2, 3)),
)
NUMBER = {}
for _round in ROUNDS:
    for _m in _round:
        NUMBER[_m] = len(NUMBER)
MESSAGES = len(NUMBER)
SENT_FROM = {}
for _m in NUMBER:
    SENT_FROM.setdefault((_m[0], _m[2]), []).append(_m)

FEAT, COT, BIAS, PART, AGG, GRAD, OUT, WEIGHT, FINAL, END = 0, 4, 7, 10, 14, 18, 22, 23, 31, 35
CONTRACT_LAST = (((1,), (1,)), ((), ()))


def choose(i, values):
    chosen = jnp.int32(values[0])
    for n, value in enumerate(values[1:], 1):
        chosen = jnp.where(i == n, jnp.int32(value), chosen)
    return chosen


def kernel(
    dst_ids,
    src_ids,
    counts,
    feat,
    cot,
    weight,
    bias,
    edge,
    out_ref,
    gin_ref,
    gw_ref,
    gb_ref,
    blocks,
    gathered,
    acc,
    cot_all,
    bias_got,
    bias_col,
    weight_t,
    part_got,
    agg,
    pre_grad,
    grad_agg,
    out_half,
    out_got,
    wterm,
    wcore,
    wlink,
    wy,
    wz,
    part,
    own_part,
    shares,
    shares_got,
    final,
    final_got,
    lists,
    slots,
    list_sem,
    edge_sem,
    send_sem,
    gather_sem,
    scatter_sem,
    odd_send,
    odd_recv,
):
    row, col = lax.axis_index("row"), lax.axis_index("col")
    y, a, z = row // 8, (row // 4) % 2, row % 4
    hi, b = col // 2, col % 2
    nslot = 16

    def device(yy, aa, zz, hh, bb):
        return ((yy * 2 + aa) * 4 + zz, hh * 2 + bb)

    def step(way):
        return device((y + way[0] + 4) % 4, a, (z + way[1] + 4) % 4, hi, b)

    def panel_of(slot):
        return (((y + slot // 4) % 4) * 2 + b) * 4 + (z + slot % 4) % 4

    def rows64(core):
        return pl.ds(pl.multiple_of(core * 64, 64), 64)

    def remote(src, dst, n_send, n_recv, target):
        return pltpu.make_async_remote_copy(
            src_ref=src,
            dst_ref=dst,
            send_sem=odd_send.at[n_send],
            recv_sem=odd_recv.at[n_recv],
            device_id=target,
            device_id_type=MESH,
        )

    partners = [device(y, 1 - a, z, hi, b), device(y, a, z, hi, 1 - b), device(y, 1 - a, z, hi, 1 - b)]
    partners += [device(y, a, z, 1 - hi, 0), device(y, a, z, 1 - hi, 1)]
    partners += [device((y + k) % 4, a, z, hi, b) for k in (1, 2, 3)]
    partners += [device(y, a, (z + k) % 4, hi, b) for k in (1, 2, 3)]
    barrier = pltpu.get_barrier_semaphore()
    for partner in partners:
        pl.semaphore_signal(barrier, inc=1, device_id=partner, device_id_type=MESH)

    loads = [
        pltpu.make_async_copy(
            edge.at[panel_of(s)], blocks.at[s, pl.ds(0, nslot)], edge_sem.at[s]
        )
        for s in range(nslot)
    ]
    for load in loads:
        load.start()

    k_of = lax.broadcasted_iota(jnp.int32, (nslot, 32), 0)
    cell = jnp.where(k_of < counts[...], dst_ids[...] * 8 + src_ids[...], -1)
    place = lax.broadcasted_iota(jnp.int32, (64, 32), 0)
    found = jnp.full((64, 32), nslot, jnp.int32)
    before = jnp.full((nslot, 32), nslot, jnp.int32)
    for k in range(nslot):
        before = jnp.where((cell == cell[k : k + 1, :]) & (k_of > k) & (cell >= 0), k, before)
        found = jnp.where(place == cell[k : k + 1, :], k, found)
    lists[...] = jnp.zeros_like(lists)
    lists[:64, :32] = found
    lists[64:, :32] = before
    list_copy = pltpu.make_async_copy(lists, slots, list_sem)
    list_copy.start()

    bias_row = bias[...]
    bias_got[col] = jnp.broadcast_to(jnp.concatenate([bias_row, bias_row], axis=1), (8, 128))
    pl.semaphore_wait(barrier, len(partners))

    def feature_copy(half, chip, core_from, target):
        return remote(
            feat.at[:, pl.ds(half * 512, 512)],
            gathered.at[half, 0, rows64(core_from)],
            FEAT + 2 * half + chip,
            FEAT + 2 * half + core_from,
            target,
        )

    for half in range(2):
        for chip in range(2):
            here = jnp.logical_and(a == chip, a == b)

            @pl.when(jnp.logical_not(here))
            def _():
                feature_copy(half, chip, b, device(y, chip, z, hi, a)).start()

            @pl.when(here)
            def _():
                gathered[half, 0, rows64(b), :] = feat[:, half * 512 : half * 512 + 512]

    def feature_landed(half):
        for core in range(2):

            @pl.when(jnp.logical_not(jnp.logical_and(a == b, core == b)))
            def _():
                feature_copy(half, 0, core, device(y, 1 - a, z, hi, b)).wait_recv()

    def gather_copy(m):
        half, way, start, end = m
        return pltpu.make_async_remote_copy(
            src_ref=gathered.at[half, start],
            dst_ref=gathered.at[half, end],
            send_sem=send_sem.at[NUMBER[m]],
            recv_sem=gather_sem.at[NUMBER[m]],
            device_id=step(way),
            device_id_type=MESH,
        )

    def cot_copy(k):
        other = (col + k) % 4
        return remote(
            cot.at[:, pl.ds(pl.multiple_of((other % 2) * 512, 512), 512)],
            cot_all.at[rows64(col)],
            COT + k - 1,
            COT + k - 1,
            (row, other),
        )

    def cot_landed(k):
        return remote(
            cot.at[:, pl.ds(0, 512)],
            cot_all.at[rows64((col + 4 - k) % 4)],
            COT + k - 1,
            COT + k - 1,
            (row, (col + k) % 4),
        )

    def bias_copy(k, place):
        return remote(bias_got.at[col], bias_got.at[place], BIAS + k - 1, BIAS + k - 1, (row, (col + k) % 4))

    for half in range(2):
        feature_landed(half)
        for m in ROUNDS[half]:
            gather_copy(m).start()
    for k in (1, 2, 3):
        cot_copy(k).start()
        bias_copy(k, col).start()
    cot_all[rows64(col), :] = cot[:, pl.ds(pl.multiple_of(b * 512, 512), 512)]

    acc[...] = jnp.zeros_like(acc)
    weight_t[...] = weight[...].T
    list_copy.wait()
    for load in loads:
        load.wait()

    def merge(s, _):
        j = panel_of(s)
        blocks[s, nslot] = jnp.zeros((128, 128), BF)
        for k in range(1, nslot):
            blocks[s, k] = blocks[s, k] + blocks[s, slots[64 + k, j]]
        return 0

    lax.fori_loop(0, nslot, merge, 0)

    def forward_units(units):
        def one(i, _):
            half = choose(i, [u[0] for u in units])
            slot = choose(i, [u[1] for u in units])
            j, at = panel_of(slot), 4 * half
            x = gathered[half, slot]
            for q in range(4):
                placed = jnp.concatenate(
                    [
                        jnp.concatenate([blocks[slot, slots[at + 8 * d + s, j]] for s in range(4)], axis=1)
                        for d in (2 * q, 2 * q + 1)
                    ],
                    axis=0,
                )
                acc[:, 256 * q : 256 * q + 256] += lax.dot_general(
                    x, placed, CONTRACT_LAST, preferred_element_type=F32
                )
            return 0

        lax.fori_loop(0, len(units), one, 0)

    forward_units(((0, 0), (1, 0)))
    for k, now in enumerate(ROUNDS):
        for m in now:
            gather_copy(m).wait_recv()
        if k + 2 < len(ROUNDS):
            for m in ROUNDS[k + 2]:
                gather_copy(m).start()
        forward_units([(m[0], m[3]) for m in now])
        if k == 4:
            for other in (1, 2, 3):
                cot_landed(other).wait_recv()
                bias_copy(other, (col + 4 - other) % 4).wait_recv()
            for h in range(2):
                lanes = jnp.concatenate([bias_got[2 * h][0:1, :64], bias_got[2 * h + 1][0:1, :64]], axis=1)
                bias_col[h * 128 : h * 128 + 128, :] = jnp.broadcast_to(lanes, (128, 128)).T

    sibling = device(y, a, z, hi, 1 - b)
    peer = device(y, a, z, 1 - hi, b)
    own_rows = pl.ds(pl.multiple_of(hi * 128, 128), 128)
    peer_rows = pl.ds(pl.multiple_of(128 - hi * 128, 128), 128)

    def lanes(t):
        return pl.ds(t * 128, 128)

    def part_copy(t):
        theirs = pl.ds(pl.multiple_of((1 - b) * 512 + t * 128, 128), 128)
        return remote(acc.at[:, theirs], part_got.at[t], PART + t, PART + t, sibling)

    def agg_copy(t, rows):
        return remote(agg.at[own_rows, lanes(t)], agg.at[rows, lanes(t)], AGG + t, AGG + t, peer)

    def grad_copy(t, core):
        return remote(grad_agg.at[4 * b + t], grad_agg.at[4 * core + t], GRAD + t, GRAD + t, sibling)

    for t in range(4):
        part_copy(t).start()
    for t in range(4):
        part_copy(t).wait_recv()
        mine = pl.ds(pl.multiple_of(b * 512 + t * 128, 128), 128)
        agg[own_rows, lanes(t)] = (acc[:, mine] + part_got[t]).astype(BF)
        agg_copy(t, own_rows).start()
    for m in NUMBER:
        gather_copy(m).wait_send()
    for t in range(4):
        agg_copy(t, peer_rows).wait_recv()
        pre = jnp.dot(weight_t[...], agg[:, lanes(t)], preferred_element_type=F32) + bias_col[...]
        sig = jax.nn.sigmoid(pre)
        value = pre * sig
        grad = (cot_all[:, lanes(t)].astype(F32) * sig * (1.0 + pre * (1.0 - sig))).astype(BF)
        pre_grad[:, lanes(t)] = grad
        grad_agg[4 * b + t] = jnp.dot(weight[own_rows, :], grad, preferred_element_type=F32).astype(BF)
        grad_copy(t, b).start()
        out_half[:, lanes(t)] = jnp.where(hi == 0, value[:128], value[128:]).astype(BF)
    out_copy = remote(out_half.at[rows64(1 - b)], out_got, OUT, OUT, sibling)
    out_copy.start()

    term = lax.dot_general(agg[own_rows, :], pre_grad[...], CONTRACT_LAST, preferred_element_type=F32)
    bias_term = lax.dot_general(jnp.ones((16, 512), BF), pre_grad[...], CONTRACT_LAST, preferred_element_type=F32)
    for core in range(2):
        wterm[core, :64] = term[core * 64 : core * 64 + 64, :]
        wterm[core, 64:] = bias_term
    weight_core = remote(wterm.at[1 - b], wcore, WEIGHT, WEIGHT, sibling)
    weight_core.start()
    weight_link = remote(wlink.at[0], wlink.at[1], WEIGHT + 1, WEIGHT + 1, device(y, 1 - a, z, hi, b))

    def weight_y(k, place):
        return remote(
            wy.at[y], wy.at[place], WEIGHT + 1 + k, WEIGHT + 1 + k, device((y + k) % 4, a, z, hi, b)
        )

    def weight_z(k, place):
        return remote(
            wz.at[z], wz.at[place], WEIGHT + 4 + k, WEIGHT + 4 + k, device(y, a, (z + k) % 4, hi, b)
        )

    def scatter_copy(m):
        half, way, start, end = m
        return pltpu.make_async_remote_copy(
            src_ref=shares.at[half, end],
            dst_ref=shares_got.at[NUMBER[m]],
            send_sem=send_sem.at[NUMBER[m]],
            recv_sem=scatter_sem.at[NUMBER[m]],
            device_id=step((-way[0], -way[1])),
            device_id_type=MESH,
        )

    def backward_units(units, result):
        def one(i, _):
            half = choose(i, [u[0] for u in units])
            slot = choose(i, [u[1] for u in units])
            j, at = panel_of(slot), 4 * half
            grads = jnp.concatenate([grad_agg[d] for d in range(8)], axis=1)
            for s in (0, 2):
                placed = jnp.concatenate(
                    [
                        jnp.concatenate([blocks[slot, slots[at + 8 * d + s + e, j]] for e in (0, 1)], axis=1)
                        for d in range(8)
                    ],
                    axis=0,
                )
                result[i, :, s * 128 : s * 128 + 256] = jnp.dot(
                    grads, placed, preferred_element_type=F32
                )
            return 0

        lax.fori_loop(0, len(units), one, 0)

    def with_arrivals(half, slot, result, i):
        total = result[i]
        for m in SENT_FROM.get((half, slot), ()):
            scatter_copy(m).wait_recv()
            total = total + shares_got[NUMBER[m]].astype(F32)
        return total.astype(BF)

    for t in range(4):
        grad_copy(t, 1 - b).wait_recv()
    for k in range(len(ROUNDS) - 1, -1, -1):
        now = ROUNDS[k]
        backward_units([(m[0], m[3]) for m in now], part)
        for i, m in enumerate(now):
            shares[m[0], m[3]] = with_arrivals(m[0], m[3], part, i)
            scatter_copy(m).start()
        if k == 7:
            weight_core.wait_recv()
            wlink[0] = wterm[b] + wcore[...]
            weight_link.start()
        if k == 5:
            weight_link.wait_recv()
            wy[y] = (wlink[0] + wlink[1]).astype(BF)
            for n in (1, 2, 3):
                weight_y(n, y).start()
        if k == 2:
            for n in (1, 2, 3):
                weight_y(n, (y + 4 - n) % 4).wait_recv()
            wz[z] = sum(wy[n].astype(F32) for n in range(4)).astype(BF)
            for n in (1, 2, 3):
                weight_z(n, z).start()

    backward_units(((0, 0), (1, 0)), own_part)
    out_copy.wait_recv()
    for half in range(2):
        at = slice(half * 512, half * 512 + 512)
        out_ref[:, at] = jnp.where(b == half, out_half[rows64(b), :], out_got[...])

    def final_copy(half, core, chip_from, target):
        lane = pl.ds(half * 512, 512)
        return remote(
            final.at[half, pl.ds(core * 64, 64)],
            final_got.at[chip_from, :, lane],
            FINAL + 2 * half + core,
            FINAL + 2 * half + chip_from,
            target,
        )

    for half in (1, 0):
        final[half] = with_arrivals(half, 0, own_part, half)
        for core in range(2):
            here = jnp.logical_and(a == b, b == core)

            @pl.when(jnp.logical_not(here))
            def _():
                final_copy(half, core, a, device(y, b, z, hi, core)).start()

            @pl.when(here)
            def _():
                final_got[a, :, half * 512 : half * 512 + 512] = final[half, core * 64 : core * 64 + 64, :]

    for n in (1, 2, 3):
        weight_z(n, (z + 4 - n) % 4).wait_recv()
    scale = 1.0 / (32 * 1024) ** 0.5
    whole = sum(wz[n].astype(F32) for n in range(4)) * scale
    gw_ref[...] = whole[:64, :]
    gb = whole[64:65, :]
    own = jnp.where(hi == 0, gb[:, :128], gb[:, 128:])
    gb_ref[...] = jnp.where(b == 0, own[:, :64], own[:, 64:])

    for half in (1, 0):
        for chip in range(2):

            @pl.when(jnp.logical_not(jnp.logical_and(a == b, chip == a)))
            def _():
                final_copy(half, 0, chip, device(y, 1 - a, z, hi, b)).wait_recv()

        at = slice(half * 512, half * 512 + 512)
        gin_ref[:, at] = (final_got[0, :, at].astype(F32) + final_got[1, :, at].astype(F32)).astype(BF)

    for half in range(2):
        for chip in range(2):

            @pl.when(jnp.logical_not(jnp.logical_and(a == chip, a == b)))
            def _():
                feature_copy(half, chip, b, device(y, chip, z, hi, a)).wait_send()

            @pl.when(jnp.logical_not(jnp.logical_and(a == b, b == chip)))
            def _():
                final_copy(half, chip, a, device(y, b, z, hi, chip)).wait_send()

    for k in (1, 2, 3):
        cot_copy(k).wait_send()
        bias_copy(k, col).wait_send()
        weight_y(k, y).wait_send()
        weight_z(k, z).wait_send()
    for t in range(4):
        part_copy(t).wait_send()
        agg_copy(t, own_rows).wait_send()
        grad_copy(t, b).wait_send()
    out_copy.wait_send()
    weight_core.wait_send()
    weight_link.wait_send()
    for m in NUMBER:
        scatter_copy(m).wait_send()


def hand_over(*refs):
    half = len(refs) // 2
    for n in range(half):
        refs[half + n][...] = refs[n][...]


def body(features, weight, bias, edge_blocks, block_dst, block_src, counts, cotangent):
    vmem = pl.BlockSpec(memory_space=pltpu.VMEM)
    out, gin, gw, gb = pl.pallas_call(
        kernel,
        out_shape=(
            jax.ShapeDtypeStruct((64, 1024), BF),
            jax.ShapeDtypeStruct((64, 1024), BF),
            jax.ShapeDtypeStruct((64, 256), F32),
            jax.ShapeDtypeStruct((1, 64), F32),
        ),
        in_specs=[vmem, vmem, vmem, vmem, vmem, vmem, vmem, pl.BlockSpec(memory_space=pl.ANY)],
        out_specs=(vmem, vmem, vmem, vmem),
        scratch_shapes=[
            pltpu.VMEM((16, 17, 128, 128), BF),
            pltpu.VMEM((2, 16, 128, 512), BF),
            pltpu.VMEM((128, 1024), F32),
            pltpu.VMEM((256, 512), BF),
            pltpu.VMEM((4, 8, 128), F32),
            pltpu.VMEM((256, 128), F32),
            pltpu.VMEM((256, 256), BF),
            pltpu.VMEM((4, 128, 128), F32),
            pltpu.VMEM((256, 512), BF),
            pltpu.VMEM((256, 512), BF),
            pltpu.VMEM((8, 128, 128), BF),
            pltpu.VMEM((128, 512), BF),
            pltpu.VMEM((64, 512), BF),
            pltpu.VMEM((2, 80, 256), F32),
            pltpu.VMEM((80, 256), F32),
            pltpu.VMEM((2, 80, 256), F32),
            pltpu.VMEM((4, 80, 256), BF),
            pltpu.VMEM((4, 80, 256), BF),
            pltpu.VMEM((4, 128, 512), F32),
            pltpu.VMEM((2, 128, 512), F32),
            pltpu.VMEM((2, 16, 128, 512), BF),
            pltpu.VMEM((MESSAGES, 128, 512), BF),
            pltpu.VMEM((2, 128, 512), BF),
            pltpu.VMEM((2, 64, 1024), BF),
            pltpu.VMEM((80, 128), jnp.int32),
            pltpu.SMEM((80, 128), jnp.int32),
            pltpu.SemaphoreType.DMA,
            pltpu.SemaphoreType.DMA((16,)),
            pltpu.SemaphoreType.DMA((MESSAGES,)),
            pltpu.SemaphoreType.DMA((MESSAGES,)),
            pltpu.SemaphoreType.DMA((MESSAGES,)),
            pltpu.SemaphoreType.DMA((END,)),
            pltpu.SemaphoreType.DMA((END,)),
        ],
        compiler_params=pltpu.CompilerParams(
            collective_id=0, has_side_effects=True, vmem_limit_bytes=56 * 1024 * 1024
        ),
        name="graph_layer",
    )(block_dst[0].T, block_src[0].T, counts, features.T, cotangent.T, weight, bias.reshape(1, 64), edge_blocks[0])
    results = (out, gin, gw, gb)
    out, gin, gw, gb = pl.pallas_call(
        hand_over,
        out_shape=tuple(jax.ShapeDtypeStruct(x.shape, x.dtype) for x in results),
        in_specs=[vmem] * 4,
        out_specs=(vmem,) * 4,
        name="hand_over",
    )(*results)
    return out.T, gin.T, gw, gb.reshape(64)


def solution(mesh):
    return jax.shard_map(
        body,
        mesh=mesh,
        in_specs=(
            P("row", "col"),
            P(),
            P("col"),
            P("row", None, None, None, None),
            P("row", None, None),
            P("row", None, None),
            P("row", None),
            P("row", "col"),
        ),
        out_specs=(P("row", "col"), P("row", "col"), P("col", None), P("col")),
        check_vma=False,
    )
```

time: 1650 us -> 80.8 us (0.05); the launches traced: 1620 us -> 80.6 us
  waiting for transfers between devices: 511 us -> 0 us
  local copies, waits for them, and re-layouts: 443 us -> 0 us
  blocking collectives: 426 us -> 0 us
  loops' own time: 112 us -> 0 us
  Pallas kernels: 0 us -> 80 us
  matrix products: 66.2 us -> 0 us
  other arithmetic: 50.5 us -> 0 us
    psum x1 -> x0, blocking collectives: 390 us -> none  [body(): grad_weight, grad_bias = lax.psum((weight_term, bias_term), 'row')]
    psum x1 -> x0, waiting for transfers between devices: 276 us -> none  [body(): grad_weight, grad_bias = lax.psum((weight_term, bias_term), 'row')]
    dynamic_update_slice x32 -> x0, local copies, waits for them, and re-layouts: 194 us -> none  [body(): lax.map(adjoint_one_panel, jnp.arange(panel_rows * lax.axis_size('row') /...]
    all_gather x1 -> x0, waiting for transfers between devices: 151 us -> none  [body(): piece = lax.all_gather(features, 'row', axis=0, tiled=True)]
    dynamic_slice x268 -> x0, local copies, waits for them, and re-layouts: 140 us -> none  [the longest x64 79.5 us: pick_slot(): return lax.dynamic_index_in_dim(table, index, 0, keepdims=False)]
    another operation x66 -> x0, loops' own time: 112 us -> none  [the longest x1 84.7 us: body(): lax.map(adjoint_one_panel, jnp.arange(panel_rows * lax.axis_size('row') /...]
    reduce_scatter x1 -> x0, waiting for transfers between devices: 83.3 us -> none  [body(): lax.psum_scatter(parts.reshape(panel_rows * lax.axis_size('row'), width_c...]
    pallas_call x0 -> x2, Pallas kernels: none -> 80 us  [the longest x1 78.3 us: body(): pl.pallas_call(kernel, out_shape=(jax.ShapeDtypeStruct((64, 1024), BF), j...]
  transfers between devices with their start and end apart: 3 -> 0, of which waited for: 3 -> 0; matrix products, arithmetic and copies ran while one was open for 0% -> 0% of each run, Pallas kernels for 0% -> 0%
where the time goes in v2:
time: 80.8 us; the launch traced here: 80.6 us
  Pallas kernels  80 us (99%)
    pallas_call x1, Pallas kernels, body(): pl.pallas_call(kernel, out_shape=(jax.ShapeDtypeStruct((64, 1024), BF), j...  78.3 us
    pallas_call x1, Pallas kernels, body(): pl.pallas_call(hand_over, out_shape=tuple((jax.ShapeDtypeStruct(x.shape,...  1.7 us

profile of v2, /device:TPU:1, one launch (start us, length us, event | category | flops | bytes accessed | tf_op | source)
XLA Modules:
  0.0 80.6 jit_solution(13803981597003302567)
XLA Ops:
  0.6 78.3 %graph_layer.1 = (bf16[64,1024]{1,0:T(8,128)(2,1)}, bf16[64,1024]{1,0:T(8,128)(2,1)}, f32[64,256]{1,0:T(8,128)}, f32[1,64]{1,0:T(1,128)}) custom-call(s32[16,32]{1,0:T(8,128)} %bitcast.16, s32[16,32]{1,0:T(8,128)} %bitcast.17, s32[1,32]{1,0:T(1,128)} %counts.1, bf16[64,1024]{1,0:T(8,128)(2,1)} %bitcast.14, bf16[64,1024]{1,0:T(8,128)(2,1)} %bitcast.15, ...), custom_call_target="tpu_custom_call" | custom-call | tf_op jit(solution)/shard_map/graph_layer/pallas_call | solution.py:487
  78.9 1.7 %hand_over.1 = (bf16[64,1024]{1,0:T(8,128)(2,1)}, bf16[64,1024]{1,0:T(8,128)(2,1)}, f32[64,256]{1,0:T(8,128)}, f32[1,64]{1,0:T(1,128)}) custom-call(bf16[64,1024]{1,0:T(8,128)(2,1)} %get-tuple-element.12.refs_0_, bf16[64,1024]{1,0:T(8,128)(2,1)} %get-tuple-element.13.refs_1_, f32[64,256]{1,0:T(8,128)} %get-tuple-element.14.refs_2_, ...), custom_call_target="tpu_custom_call" | custom-call | tf_op jit(solution)/shard_map/hand_over/pallas_call | solution.py:538

commit v3 on v2

--- a/solution.py
+++ b/solution.py
@@ -33,10 +33,18 @@
     for _m in _round:
         NUMBER[_m] = len(NUMBER)
 MESSAGES = len(NUMBER)
+PIECES = 2
+ROWS = 128 // PIECES
 SENT_FROM = {}
 for _m in NUMBER:
     SENT_FROM.setdefault((_m[0], _m[2]), []).append(_m)
 
+LEAVES = tuple(
+    m
+    for now in ROUNDS[:6]
+    for m in now
+    if (m[0], m[3]) not in SENT_FROM and m != _message(0, ZM, 1, 1)
+)
 FEAT, COT, BIAS, PART, AGG, GRAD, OUT, WEIGHT, FINAL, END = 0, 4, 7, 10, 14, 18, 22, 23, 31, 35
 CONTRACT_LAST = (((1,), (1,)), ((), ()))
 
@@ -87,7 +95,12 @@
     final_got,
     lists,
     slots,
+    link_got,
+    leaf_part,
     list_sem,
+    link_send,
+    link_recv,
+    link_back,
     edge_sem,
     send_sem,
     gather_sem,
@@ -99,6 +112,15 @@
     y, a, z = row // 8, (row // 4) % 2, row % 4
     hi, b = col // 2, col % 2
     nslot = 16
+    diag = a == b
+    off_diag = jnp.logical_not(diag)
+
+    def unless_leaf(m, run):
+        if m in LEAVES:
+            pl.when(diag)(run)
+        else:
+            run()
+
 
     def device(yy, aa, zz, hh, bb):
         return ((yy * 2 + aa) * 4 + zz, hh * 2 + bb)
@@ -185,14 +207,27 @@
             def _():
                 feature_copy(half, 0, core, device(y, 1 - a, z, hi, b)).wait_recv()
 
-    def gather_copy(m):
+    def gather_copy(m, piece):
         half, way, start, end = m
+        n = PIECES * NUMBER[m] + piece
+        rows = pl.ds(piece * ROWS, ROWS)
         return pltpu.make_async_remote_copy(
-            src_ref=gathered.at[half, start],
-            dst_ref=gathered.at[half, end],
-            send_sem=send_sem.at[NUMBER[m]],
-            recv_sem=gather_sem.at[NUMBER[m]],
+            src_ref=gathered.at[half, start, rows],
+            dst_ref=gathered.at[half, end, rows],
+            send_sem=send_sem.at[n],
+            recv_sem=gather_sem.at[n],
             device_id=step(way),
+            device_id_type=MESH,
+        )
+
+    def link_copy(m):
+        n = LEAVES.index(m)
+        return pltpu.make_async_remote_copy(
+            src_ref=gathered.at[m[0], m[3]],
+            dst_ref=gathered.at[m[0], m[3]],
+            send_sem=link_send.at[n],
+            recv_sem=link_recv.at[n],
+            device_id=device(y, 1 - a, z, hi, b),
             device_id_type=MESH,
         )
 
@@ -220,8 +255,9 @@
 
     for half in range(2):
         feature_landed(half)
-        for m in ROUNDS[half]:
-            gather_copy(m).start()
+        for piece in range(PIECES):
+            for m in ROUNDS[half]:
+                unless_leaf(m, lambda: gather_copy(m, piece).start())
     for k in (1, 2, 3):
         cot_copy(k).start()
         bias_copy(k, col).start()
@@ -261,16 +297,40 @@
                 )
             return 0
 
-        lax.fori_loop(0, len(units), one, 0)
+        if units:
+            lax.fori_loop(0, len(units), one, 0)
 
     forward_units(((0, 0), (1, 0)))
+    def leaves_of(k):
+        return [m for m in ROUNDS[k] if m in LEAVES] if k >= 0 else []
+
+    def wait_leaves(leaves):
+        for m in leaves:
+            link_copy(m).wait_recv()
+
+    def pass_leaves(leaves):
+        for m in leaves:
+            link_copy(m).start()
+
+    last = len(ROUNDS) - 1
+    behind = []
     for k, now in enumerate(ROUNDS):
-        for m in now:
-            gather_copy(m).wait_recv()
-        if k + 2 < len(ROUNDS):
-            for m in ROUNDS[k + 2]:
-                gather_copy(m).start()
-        forward_units([(m[0], m[3]) for m in now])
+        late = leaves_of(k - 2)
+        units = [(m[0], m[3]) for m in now if m not in LEAVES]
+        for piece in range(PIECES):
+            for m in now:
+                unless_leaf(m, lambda: gather_copy(m, piece).wait_recv())
+            if k + 2 < len(ROUNDS):
+                for m in ROUNDS[k + 2]:
+                    unless_leaf(m, lambda: gather_copy(m, piece).start())
+            if piece == 0:
+                if late:
+                    pl.when(off_diag)(lambda: wait_leaves(late))
+                forward_units(behind + [(m[0], m[3]) for m in late])
+        if leaves_of(k):
+            pl.when(diag)(lambda: pass_leaves(leaves_of(k)))
+        forward_units(units[:2])
+        behind = units[2:]
         if k == 4:
             for other in (1, 2, 3):
                 cot_landed(other).wait_recv()
@@ -278,6 +338,8 @@
             for h in range(2):
                 lanes = jnp.concatenate([bias_got[2 * h][0:1, :64], bias_got[2 * h + 1][0:1, :64]], axis=1)
                 bias_col[h * 128 : h * 128 + 128, :] = jnp.broadcast_to(lanes, (128, 128)).T
+
+    forward_units(behind)
 
     sibling = device(y, a, z, hi, 1 - b)
     peer = device(y, a, z, 1 - hi, b)
@@ -305,7 +367,14 @@
         agg[own_rows, lanes(t)] = (acc[:, mine] + part_got[t]).astype(BF)
         agg_copy(t, own_rows).start()
     for m in NUMBER:
-        gather_copy(m).wait_send()
+        for piece in range(PIECES):
+            unless_leaf(m, lambda: gather_copy(m, piece).wait_send())
+
+    def links_sent(copy):
+        for m in LEAVES:
+            copy(m).wait_send()
+
+    pl.when(diag)(lambda: links_sent(link_copy))
     for t in range(4):
         agg_copy(t, peer_rows).wait_recv()
         pre = jnp.dot(weight_t[...], agg[:, lanes(t)], preferred_element_type=F32) + bias_col[...]
@@ -338,14 +407,27 @@
             wz.at[z], wz.at[place], WEIGHT + 4 + k, WEIGHT + 4 + k, device(y, a, (z + k) % 4, hi, b)
         )
 
-    def scatter_copy(m):
+    def scatter_copy(m, piece):
         half, way, start, end = m
+        n = PIECES * NUMBER[m] + piece
+        rows = pl.ds(piece * ROWS, ROWS)
         return pltpu.make_async_remote_copy(
-            src_ref=shares.at[half, end],
-            dst_ref=shares_got.at[NUMBER[m]],
-            send_sem=send_sem.at[NUMBER[m]],
-            recv_sem=scatter_sem.at[NUMBER[m]],
+            src_ref=shares.at[half, end, rows],
+            dst_ref=shares_got.at[NUMBER[m], rows],
+            send_sem=send_sem.at[n],
+            recv_sem=scatter_sem.at[n],
             device_id=step((-way[0], -way[1])),
+            device_id_type=MESH,
+        )
+
+    def link_share(m):
+        n = LEAVES.index(m)
+        return pltpu.make_async_remote_copy(
+            src_ref=shares.at[m[0], m[3]],
+            dst_ref=link_got.at[n],
+            send_sem=link_send.at[n],
+            recv_sem=link_back.at[n],
+            device_id=device(y, 1 - a, z, hi, b),
             device_id_type=MESH,
         )
 
@@ -370,21 +452,59 @@
 
         lax.fori_loop(0, len(units), one, 0)
 
-    def with_arrivals(half, slot, result, i):
-        total = result[i]
-        for m in SENT_FROM.get((half, slot), ()):
-            scatter_copy(m).wait_recv()
-            total = total + shares_got[NUMBER[m]].astype(F32)
-        return total.astype(BF)
+    def add_up(half, slot, result, into, piece):
+        came = [m for m in SENT_FROM.get((half, slot), ()) if m not in LEAVES]
+        leaves = [m for m in SENT_FROM.get((half, slot), ()) if m in LEAVES]
+        rows = slice(piece * ROWS, piece * ROWS + ROWS)
+
+        def add_leaves():
+            for m in leaves:
+                scatter_copy(m, piece).wait_recv()
+                result[rows, :] += shares_got[NUMBER[m], rows, :].astype(F32)
+
+        if leaves:
+            pl.when(diag)(add_leaves)
+        for m in came:
+            scatter_copy(m, piece).wait_recv()
+        total = result[rows, :]
+        for m in came:
+            total = total + shares_got[NUMBER[m], rows, :].astype(F32)
+        into[rows, :] = total.astype(BF)
 
     for t in range(4):
         grad_copy(t, 1 - b).wait_recv()
-    for k in range(len(ROUNDS) - 1, -1, -1):
-        now = ROUNDS[k]
+    def backward_leaves(k):
+        leaves = [m for m in ROUNDS[k] if m in LEAVES]
+        if leaves:
+            first = LEAVES.index(leaves[0])
+            backward_units([(m[0], m[3]) for m in leaves], leaf_part.at[pl.ds(first, len(leaves))])
+
+            def give():
+                for m in leaves:
+                    shares[m[0], m[3]] = leaf_part[LEAVES.index(m)].astype(BF)
+                    link_share(m).start()
+
+            pl.when(off_diag)(give)
+
+    def send_leaf(m):
+        n = LEAVES.index(m)
+        link_share(m).wait_recv()
+        shares[m[0], m[3]] = (leaf_part[n] + link_got[n].astype(F32)).astype(BF)
+        for piece in range(PIECES):
+            scatter_copy(m, piece).start()
+
+    for k in range(last, -1, -1):
+        now = [m for m in ROUNDS[k] if m not in LEAVES]
         backward_units([(m[0], m[3]) for m in now], part)
-        for i, m in enumerate(now):
-            shares[m[0], m[3]] = with_arrivals(m[0], m[3], part, i)
-            scatter_copy(m).start()
+        for piece in range(PIECES):
+            for i, m in enumerate(now):
+                add_up(m[0], m[3], part.at[i], shares.at[m[0], m[3]], piece)
+                scatter_copy(m, piece).start()
+        for m in ROUNDS[k]:
+            if m in LEAVES:
+                pl.when(diag)(lambda: send_leaf(m))
+        if k >= 2:
+            backward_leaves(k - 2)
         if k == 7:
             weight_core.wait_recv()
             wlink[0] = wterm[b] + wcore[...]
@@ -418,7 +538,8 @@
         )
 
     for half in (1, 0):
-        final[half] = with_arrivals(half, 0, own_part, half)
+        for piece in range(PIECES):
+            add_up(half, 0, own_part.at[half], final.at[half], piece)
         for core in range(2):
             here = jnp.logical_and(a == b, b == core)
 
@@ -429,25 +550,6 @@
             @pl.when(here)
             def _():
                 final_got[a, :, half * 512 : half * 512 + 512] = final[half, core * 64 : core * 64 + 64, :]
-
-    for n in (1, 2, 3):
-        weight_z(n, (z + 4 - n) % 4).wait_recv()
-    scale = 1.0 / (32 * 1024) ** 0.5
-    whole = sum(wz[n].astype(F32) for n in range(4)) * scale
-    gw_ref[...] = whole[:64, :]
-    gb = whole[64:65, :]
-    own = jnp.where(hi == 0, gb[:, :128], gb[:, 128:])
-    gb_ref[...] = jnp.where(b == 0, own[:, :64], own[:, 64:])
-
-    for half in (1, 0):
-        for chip in range(2):
-
-            @pl.when(jnp.logical_not(jnp.logical_and(a == b, chip == a)))
-            def _():
-                final_copy(half, 0, chip, device(y, 1 - a, z, hi, b)).wait_recv()
-
-        at = slice(half * 512, half * 512 + 512)
-        gin_ref[:, at] = (final_got[0, :, at].astype(F32) + final_got[1, :, at].astype(F32)).astype(BF)
 
     for half in range(2):
         for chip in range(2):
@@ -473,7 +575,28 @@
     weight_core.wait_send()
     weight_link.wait_send()
     for m in NUMBER:
-        scatter_copy(m).wait_send()
+        for piece in range(PIECES):
+            unless_leaf(m, lambda: scatter_copy(m, piece).wait_send())
+    pl.when(off_diag)(lambda: links_sent(link_share))
+
+    for n in (1, 2, 3):
+        weight_z(n, (z + 4 - n) % 4).wait_recv()
+    scale = 1.0 / (32 * 1024) ** 0.5
+    whole = sum(wz[n].astype(F32) for n in range(4)) * scale
+    gw_ref[...] = whole[:64, :]
+    gb = whole[64:65, :]
+    own = jnp.where(hi == 0, gb[:, :128], gb[:, 128:])
+    gb_ref[...] = jnp.where(b == 0, own[:, :64], own[:, 64:])
+
+    for half in (1, 0):
+        for chip in range(2):
+
+            @pl.when(jnp.logical_not(jnp.logical_and(a == b, chip == a)))
+            def _():
+                final_copy(half, 0, chip, device(y, 1 - a, z, hi, b)).wait_recv()
+
+        at = slice(half * 512, half * 512 + 512)
+        gin_ref[:, at] = (final_got[0, :, at].astype(F32) + final_got[1, :, at].astype(F32)).astype(BF)
 
 
 def hand_over(*refs):
@@ -521,11 +644,16 @@
             pltpu.VMEM((2, 64, 1024), BF),
             pltpu.VMEM((80, 128), jnp.int32),
             pltpu.SMEM((80, 128), jnp.int32),
+            pltpu.VMEM((len(LEAVES), 128, 512), BF),
+            pltpu.VMEM((len(LEAVES), 128, 512), F32),
             pltpu.SemaphoreType.DMA,
+            pltpu.SemaphoreType.DMA((len(LEAVES),)),
+            pltpu.SemaphoreType.DMA((len(LEAVES),)),
+            pltpu.SemaphoreType.DMA((len(LEAVES),)),
             pltpu.SemaphoreType.DMA((16,)),
-            pltpu.SemaphoreType.DMA((MESSAGES,)),
-            pltpu.SemaphoreType.DMA((MESSAGES,)),
-            pltpu.SemaphoreType.DMA((MESSAGES,)),
+            pltpu.SemaphoreType.DMA((PIECES * MESSAGES,)),
+            pltpu.SemaphoreType.DMA((PIECES * MESSAGES,)),
+            pltpu.SemaphoreType.DMA((PIECES * MESSAGES,)),
             pltpu.SemaphoreType.DMA((END,)),
             pltpu.SemaphoreType.DMA((END,)),
         ],

time: 80.8 us -> 78.1 us (0.967)
  Pallas kernels: 80 us -> 77.3 us
    pallas_call x1, Pallas kernels: 78.3 us -> 75.6 us  [body(): pl.pallas_call(kernel, out_shape=(jax.ShapeDtypeStruct((64, 1024), BF), j...]
where the time goes in v3:
time: 78.1 us; the launch traced here: 78 us
  Pallas kernels  77.3 us (99%)
    pallas_call x1, Pallas kernels, body(): pl.pallas_call(kernel, out_shape=(jax.ShapeDtypeStruct((64, 1024), BF), j...  75.6 us
    pallas_call x1, Pallas kernels, body(): pl.pallas_call(hand_over, out_shape=tuple((jax.ShapeDtypeStruct(x.shape,...  1.7 us

profile of v3, /device:TPU:1, one launch (start us, length us, event | category | flops | bytes accessed | tf_op | source)
XLA Modules:
  0.0 78.0 jit_solution(10597752829936837801)
XLA Ops:
  0.6 75.6 %graph_layer.1 = (bf16[64,1024]{1,0:T(8,128)(2,1)}, bf16[64,1024]{1,0:T(8,128)(2,1)}, f32[64,256]{1,0:T(8,128)}, f32[1,64]{1,0:T(1,128)}) custom-call(s32[16,32]{1,0:T(8,128)} %bitcast.16, s32[16,32]{1,0:T(8,128)} %bitcast.17, s32[1,32]{1,0:T(1,128)} %counts.1, bf16[64,1024]{1,0:T(8,128)(2,1)} %bitcast.14, bf16[64,1024]{1,0:T(8,128)(2,1)} %bitcast.15, ...), custom_call_target="tpu_custom_call" | custom-call | tf_op jit(solution)/shard_map/graph_layer/pallas_call | solution.py:610
  76.3 1.7 %hand_over.1 = (bf16[64,1024]{1,0:T(8,128)(2,1)}, bf16[64,1024]{1,0:T(8,128)(2,1)}, f32[64,256]{1,0:T(8,128)}, f32[1,64]{1,0:T(1,128)}) custom-call(bf16[64,1024]{1,0:T(8,128)(2,1)} %get-tuple-element.12.refs_0_, bf16[64,1024]{1,0:T(8,128)(2,1)} %get-tuple-element.13.refs_1_, f32[64,256]{1,0:T(8,128)} %get-tuple-element.14.refs_2_, ...), custom_call_target="tpu_custom_call" | custom-call | tf_op jit(solution)/shard_map/hand_over/pallas_call | solution.py:666

commit v4 on v3

--- a/solution.py
+++ b/solution.py
@@ -253,6 +253,8 @@
     def bias_copy(k, place):
         return remote(bias_got.at[col], bias_got.at[place], BIAS + k - 1, BIAS + k - 1, (row, (col + k) % 4))
 
+    acc[...] = jnp.zeros_like(acc)
+    weight_t[...] = weight[...].T
     for half in range(2):
         feature_landed(half)
         for piece in range(PIECES):
@@ -263,8 +265,6 @@
         bias_copy(k, col).start()
     cot_all[rows64(col), :] = cot[:, pl.ds(pl.multiple_of(b * 512, 512), 512)]
 
-    acc[...] = jnp.zeros_like(acc)
-    weight_t[...] = weight[...].T
     list_copy.wait()
     for load in loads:
         load.wait()
@@ -300,7 +300,6 @@
         if units:
             lax.fori_loop(0, len(units), one, 0)
 
-    forward_units(((0, 0), (1, 0)))
     def leaves_of(k):
         return [m for m in ROUNDS[k] if m in LEAVES] if k >= 0 else []
 
@@ -313,7 +312,7 @@
             link_copy(m).start()
 
     last = len(ROUNDS) - 1
-    behind = []
+    behind = [(0, 0), (1, 0)]
     for k, now in enumerate(ROUNDS):
         late = leaves_of(k - 2)
         units = [(m[0], m[3]) for m in now if m not in LEAVES]
@@ -514,7 +513,7 @@
             wy[y] = (wlink[0] + wlink[1]).astype(BF)
             for n in (1, 2, 3):
                 weight_y(n, y).start()
-        if k == 2:
+        if k == 3:
             for n in (1, 2, 3):
                 weight_y(n, (y + 4 - n) % 4).wait_recv()
             wz[z] = sum(wy[n].astype(F32) for n in range(4)).astype(BF)

time: 78.1 us -> 79 us (1.012)
  Pallas kernels: 77.3 us -> 78.2 us
    pallas_call x1, Pallas kernels: 75.6 us -> 76.5 us  [body(): pl.pallas_call(kernel, out_shape=(jax.ShapeDtypeStruct((64, 1024), BF), j...]
where the time goes in v4:
time: 79 us; the launch traced here: 78.9 us
  Pallas kernels  78.2 us (99%)
    pallas_call x1, Pallas kernels, body(): pl.pallas_call(kernel, out_shape=(jax.ShapeDtypeStruct((64, 1024), BF), j...  76.5 us
    pallas_call x1, Pallas kernels, body(): pl.pallas_call(hand_over, out_shape=tuple((jax.ShapeDtypeStruct(x.shape,...  1.7 us

profile of v4, /device:TPU:1, one launch (start us, length us, event | category | flops | bytes accessed | tf_op | source)
XLA Modules:
  0.0 78.9 jit_solution(3693034012700395047)
XLA Ops:
  0.6 76.5 %graph_layer.1 = (bf16[64,1024]{1,0:T(8,128)(2,1)}, bf16[64,1024]{1,0:T(8,128)(2,1)}, f32[64,256]{1,0:T(8,128)}, f32[1,64]{1,0:T(1,128)}) custom-call(s32[16,32]{1,0:T(8,128)} %bitcast.16, s32[16,32]{1,0:T(8,128)} %bitcast.17, s32[1,32]{1,0:T(1,128)} %counts.1, bf16[64,1024]{1,0:T(8,128)(2,1)} %bitcast.14, bf16[64,1024]{1,0:T(8,128)(2,1)} %bitcast.15, ...), custom_call_target="tpu_custom_call" | custom-call | tf_op jit(solution)/shard_map/graph_layer/pallas_call | solution.py:609
  77.1 1.7 %hand_over.1 = (bf16[64,1024]{1,0:T(8,128)(2,1)}, bf16[64,1024]{1,0:T(8,128)(2,1)}, f32[64,256]{1,0:T(8,128)}, f32[1,64]{1,0:T(1,128)}) custom-call(bf16[64,1024]{1,0:T(8,128)(2,1)} %get-tuple-element.12.refs_0_, bf16[64,1024]{1,0:T(8,128)(2,1)} %get-tuple-element.13.refs_1_, f32[64,256]{1,0:T(8,128)} %get-tuple-element.14.refs_2_, ...), custom_call_target="tpu_custom_call" | custom-call | tf_op jit(solution)/shard_map/hand_over/pallas_call | solution.py:665
